TPU v7x, 32 devices: a whole 2x2x4 slice. The times are simulated.
32 devices in a mesh: depth: 4 (over y, x), panel: 8 (over z, core).
Axes of the slice: x: 2, y: 2, z: 4, core: 2. Of those that a mesh axis runs over, the one named last changes fastest.
Arguments:
- diag_blocks: float32 [4, 1024, 1024], P('depth', 'panel'), as said below
- coupling: float32 [4, 1024, 1024], P('depth', 'panel'), may hold values from -0.078125 to 0.078125
- sources: float32 [4, 1024, 256], P('depth', 'panel'), may hold values from -6 to 6
- requests: int32 [4, 128], P('depth', 'panel'), may hold values from 0 to 1023, as said below
Outputs:
- panels: float32 [4, 1024, 256], P('depth', 'panel')
- picked: float32 [4, 128, 256], P('depth', 'panel')
Inputs may be any that keep to these rules, and one draw needn't show every extreme that they name: `requests`: row numbers within their block; both 0 and 1023 occur. `diag_blocks`: every diagonal block is exactly symmetric with a positive diagonal.
All inputs are finite; a program needn't handle non-finite values.
Results may differ from a plain program's by a relative error of at most 0.0001.
Values sent between devices are 32-bit elements; how exact they have to be, the bound alone decides.
A program may use at most 64 MiB of HBM per device.

v0:
```python
import jax
import jax.numpy as jnp
from jax import lax
from jax.sharding import PartitionSpec as P

ITERS = 2


highest = lax.Precision.HIGHEST


def passed_along(block, axis, distance):
    devices = range(lax.axis_size(axis))
    route = [(i - distance, i) for i in devices if i - distance in devices]
    return lax.ppermute(block, axis, route)


def product_rows(matrix, panel_rows):
    initial = jnp.zeros((matrix.shape[0], panel_rows.shape[1]), jnp.float32)
    shard_rows = lax.all_gather(panel_rows, "panel", axis=0, tiled=True)
    columns = lax.slice_in_dim(matrix, 0, shard_rows.shape[0], axis=1)
    return initial + jnp.dot(
        columns, shard_rows, precision=highest, preferred_element_type=jnp.float32
    )


def product_transposed(matrix, panel_rows):
    return lax.psum_scatter(
        lax.dot_general(
            matrix,
            panel_rows,
            (((0,), (0,)), ((), ())),
            precision=highest,
            preferred_element_type=jnp.float32,
        ),
        "panel",
        scatter_dimension=0,
        tiled=True,
    )


def jacobi(matrix, diag_part, right_hand):
    scaled = diag_part[:, None]
    iterate = right_hand / scaled
    for sweep_no in range(ITERS):
        image = product_rows(matrix, iterate)
        iterate = iterate + (right_hand - image) / scaled
    return iterate


def per_device(diag_blocks, coupling, sources, requests):
    depth_count = lax.axis_size("depth")
    depth_pos = lax.axis_index("depth")
    panel_pos = lax.axis_index("panel")
    block_count = diag_blocks.shape[0]
    row_count = diag_blocks.shape[1]
    local_cols = sources.shape[2]
    own_square = lax.dynamic_slice_in_dim(diag_blocks, panel_pos * row_count, row_count, 2)
    diag_part = jnp.diagonal(own_square, axis1=1, axis2=2)
    col_groups = max(1, local_cols // 128)
    col_width = local_cols // col_groups
    section_total = depth_count + col_groups - 1
    left_terms = jnp.zeros_like(sources)
    carried = jnp.zeros((row_count, col_width), jnp.float32)
    for section_no in range(section_total):
        column_pos = section_no - depth_pos
        active = (column_pos >= 0) & (column_pos < col_groups)
        col_start = jnp.clip(column_pos, 0, col_groups - 1) * col_width
        block_no = 0
        source_cols = lax.dynamic_slice_in_dim(sources[block_no], col_start, col_width, 1)
        stored = lax.dynamic_update_slice_in_dim(left_terms[block_no], carried, col_start, 1)
        left_terms = left_terms.at[block_no].set(jnp.where(active, stored, left_terms[block_no]))
        forward = jacobi(diag_blocks[block_no], diag_part[block_no], source_cols - carried)
        carried = product_transposed(coupling[block_no], forward)
        carried = passed_along(carried, "depth", 1)
    panels = jnp.zeros_like(sources)
    ahead = jnp.zeros((row_count, col_width), jnp.float32)
    for section_no in range(section_total):
        column_pos = section_no - (depth_count - 1 - depth_pos)
        active = (column_pos >= 0) & (column_pos < col_groups)
        col_start = jnp.clip(column_pos, 0, col_groups - 1) * col_width
        for block_no in reversed(range(block_count)):
            source_cols = lax.dynamic_slice_in_dim(sources[block_no], col_start, col_width, 1)
            left_cols = lax.dynamic_slice_in_dim(left_terms[block_no], col_start, col_width, 1)
            right_term = product_rows(coupling[block_no], ahead)
            ahead = jacobi(
                diag_blocks[block_no], diag_part[block_no], source_cols - left_cols - right_term
            )
            stored = lax.dynamic_update_slice_in_dim(panels[block_no], ahead, col_start, 1)
            panels = panels.at[block_no].set(jnp.where(active, stored, panels[block_no]))
        ahead = passed_along(ahead, "depth", -1)
    picked_rows = requests.shape[1]
    shard_rows = lax.all_gather(panels, "panel", axis=1, tiled=True)
    shard_len = shard_rows.shape[1]
    inside = (requests >= 0) & (requests < shard_len)
    clipped = jnp.clip(requests, 0, shard_len - 1)
    where_rows = jnp.broadcast_to(
        clipped[:, :, None], (block_count, picked_rows, shard_rows.shape[2])
    )
    taken = jnp.take_along_axis(shard_rows, where_rows, axis=1)
    picked = jnp.where(inside[:, :, None], taken, 0.0)
    return (panels, picked)


def solution(mesh):
    placed = (
        P("depth", "panel", None),
        P("depth", "panel", None),
        P("depth", "panel", None),
        P("depth", "panel"),
    )
    return jax.shard_map(
        per_device,
        mesh=mesh,
        in_specs=placed,
        out_specs=(P("depth", "panel", None), P("depth", "panel", None)),
        check_vma=False,
    )
```

profile of v0, /device:TPU:0, one launch (start us, length us, event | category | flops | bytes accessed | tf_op | source)
XLA Modules:
  0.0 630.8 jit_solution(2935585928420736727)
XLA Ops:
  7.3 1.4 constant_dynamic-slice_fusion.1
  10.1 16.6 %all_gather.70 = f32[1024,128]{0,1:T(8,128)S(1)} all-gather(f32[128,128]{0,1:T(8,128)S(1)} %bitcast_divide_fusion), channel_id=1, replica_groups=mesh['depth'=4,'panel'=8] {'panel'}, dimensions={0}, use_global_device_ids=true | all-gather | bytes 589824 | tf_op jit(solution)/shard_map/all_gather | solution.py:20
  27.3 14.9 %all_gather.71 = f32[1024,128]{0,1:T(8,128)S(1)} all-gather(f32[128,128]{0,1:T(8,128)S(1)} %fusion.57), channel_id=1, replica_groups=mesh['depth'=4,'panel'=8] {'panel'}, dimensions={0}, use_global_device_ids=true | all-gather | bytes 589824 | tf_op jit(solution)/shard_map/all_gather | solution.py:20
  42.7 1.4 convolution_bitcast_fusion.3
  44.2 32.5 %reduce-scatter.5.cloned.1.call-done = f32[128,128]{0,1:T(8,128)} async-done(((f32[1024,128]{0,1:T(8,128)}), f32[128,128]{0,1:T(8,128)}) %reduce-scatter.5.cloned.1.call-update) | async-done | bytes 65552 | tf_op jit(solution)/shard_map/reduce_scatter | solution.py:28
  76.7 3.3 collective-permute-start
  80.1 2.1 collective-permute-done
  82.3 14.9 %all_gather.72 = f32[1024,128]{0,1:T(8,128)S(1)} all-gather(f32[128,128]{0,1:T(8,128)S(1)} %broadcast_divide_fusion.7), channel_id=1, replica_groups=mesh['depth'=4,'panel'=8] {'panel'}, dimensions={0}, use_global_device_ids=true | all-gather | bytes 589824 | tf_op jit(solution)/shard_map/all_gather | solution.py:20
  97.7 15.0 %all_gather.73 = f32[1024,128]{0,1:T(8,128)S(1)} all-gather(f32[128,128]{0,1:T(8,128)S(1)} %fusion.51), channel_id=1, replica_groups=mesh['depth'=4,'panel'=8] {'panel'}, dimensions={0}, use_global_device_ids=true | all-gather | bytes 589824 | tf_op jit(solution)/shard_map/all_gather | solution.py:20
  113.3 1.4 convolution_bitcast_fusion.2
  114.8 30.3 %reduce-scatter.7.cloned.1.call-done = f32[128,128]{0,1:T(8,128)} async-done(((f32[1024,128]{0,1:T(8,128)}), f32[128,128]{0,1:T(8,128)}) %reduce-scatter.7.cloned.1.call-update) | async-done | bytes 65552 | tf_op jit(solution)/shard_map/reduce_scatter | solution.py:28
  145.1 3.4 collective-permute-start.1
  148.5 2.1 collective-permute-done.1
  150.6 14.9 %all_gather.74 = f32[1024,128]{0,1:T(8,128)S(1)} all-gather(f32[128,128]{0,1:T(8,128)S(1)} %broadcast_divide_fusion.6), channel_id=1, replica_groups=mesh['depth'=4,'panel'=8] {'panel'}, dimensions={0}, use_global_device_ids=true | all-gather | bytes 589824 | tf_op jit(solution)/shard_map/all_gather | solution.py:20
  166.1 15.0 %all_gather.75 = f32[1024,128]{0,1:T(8,128)S(1)} all-gather(f32[128,128]{0,1:T(8,128)S(1)} %fusion.45), channel_id=1, replica_groups=mesh['depth'=4,'panel'=8] {'panel'}, dimensions={0}, use_global_device_ids=true | all-gather | bytes 589824 | tf_op jit(solution)/shard_map/all_gather | solution.py:20
  181.7 1.4 convolution_bitcast_fusion.1
  183.2 30.0 %reduce-scatter.9.cloned.1.call-done = f32[128,128]{0,1:T(8,128)} async-done(((f32[1024,128]{0,1:T(8,128)}), f32[128,128]{0,1:T(8,128)}) %reduce-scatter.9.cloned.1.call-update) | async-done | bytes 65552 | tf_op jit(solution)/shard_map/reduce_scatter | solution.py:28
  213.3 3.3 collective-permute-start.2
  216.7 2.2 collective-permute-done.2
  218.8 14.9 %all_gather.76 = f32[1024,128]{0,1:T(8,128)S(1)} all-gather(f32[128,128]{0,1:T(8,128)S(1)} %broadcast_divide_fusion.5), channel_id=1, replica_groups=mesh['depth'=4,'panel'=8] {'panel'}, dimensions={0}, use_global_device_ids=true | all-gather | bytes 589824 | tf_op jit(solution)/shard_map/all_gather | solution.py:20
  234.3 15.1 %all_gather.77 = f32[1024,128]{0,1:T(8,128)S(1)} all-gather(f32[128,128]{0,1:T(8,128)S(1)} %fusion.39), channel_id=1, replica_groups=mesh['depth'=4,'panel'=8] {'panel'}, dimensions={0}, use_global_device_ids=true | all-gather | bytes 589824 | tf_op jit(solution)/shard_map/all_gather | solution.py:20
  250.0 1.4 convolution_bitcast_fusion
  252.3 29.5 %reduce-scatter.11.cloned.1.call-done = f32[128,128]{0,1:T(8,128)} async-done(((f32[1024,128]{0,1:T(8,128)}), f32[128,128]{0,1:T(8,128)}) %reduce-scatter.11.cloned.1.call-update) | async-done | bytes 65552 | tf_op jit(solution)/shard_map/reduce_scatter | solution.py:28
  281.8 3.4 collective-permute-start.3
  285.2 2.2 collective-permute-done.3
  287.4 14.9 %all_gather.78 = f32[1024,128]{0,1:T(8,128)S(1)} all-gather(f32[128,128]{0,1:T(8,128)S(1)} %get-tuple-element.126), channel_id=1, replica_groups=mesh['depth'=4,'panel'=8] {'panel'}, dimensions={0}, use_global_device_ids=true | all-gather | bytes 589824 | tf_op jit(solution)/shard_map/all_gather | solution.py:20
  302.9 15.0 %all_gather.79 = f32[1024,128]{0,1:T(8,128)S(1)} all-gather(f32[128,128]{0,1:T(8,128)S(1)} %fusion.33), channel_id=1, replica_groups=mesh['depth'=4,'panel'=8] {'panel'}, dimensions={0}, use_global_device_ids=true | all-gather | bytes 589824 | tf_op jit(solution)/shard_map/all_gather | solution.py:20
  318.5 1.3 collective-permute-start.4
  319.8 5.5 collective-permute-done.4
  325.3 14.9 %all_gather.80 = f32[1024,128]{0,1:T(8,128)S(1)} all-gather(f32[128,128]{0,1:T(8,128)S(1)} %collective-permute-done.4), channel_id=1, replica_groups=mesh['depth'=4,'panel'=8] {'panel'}, dimensions={0}, use_global_device_ids=true | all-gather | bytes 589824 | tf_op jit(solution)/shard_map/all_gather | solution.py:20
  340.8 15.0 %all_gather.81 = f32[1024,128]{0,1:T(8,128)S(1)} all-gather(f32[128,128]{0,1:T(8,128)S(1)} %get-tuple-element.139), channel_id=1, replica_groups=mesh['depth'=4,'panel'=8] {'panel'}, dimensions={0}, use_global_device_ids=true | all-gather | bytes 589824 | tf_op jit(solution)/shard_map/all_gather | solution.py:20
  356.3 15.0 %all_gather.82 = f32[1024,128]{0,1:T(8,128)S(1)} all-gather(f32[128,128]{0,1:T(8,128)S(1)} %fusion.26), channel_id=1, replica_groups=mesh['depth'=4,'panel'=8] {'panel'}, dimensions={0}, use_global_device_ids=true | all-gather | bytes 589824 | tf_op jit(solution)/shard_map/all_gather | solution.py:20
  373.2 6.0 collective-permute-done.5
  379.2 14.9 %all_gather.83 = f32[1024,128]{0,1:T(8,128)S(1)} all-gather(f32[128,128]{0,1:T(8,128)S(1)} %collective-permute-done.5), channel_id=1, replica_groups=mesh['depth'=4,'panel'=8] {'panel'}, dimensions={0}, use_global_device_ids=true | all-gather | bytes 589824 | tf_op jit(solution)/shard_map/all_gather | solution.py:20
  394.7 15.0 %all_gather.84 = f32[1024,128]{0,1:T(8,128)S(1)} all-gather(f32[128,128]{0,1:T(8,128)S(1)} %get-tuple-element.143), channel_id=1, replica_groups=mesh['depth'=4,'panel'=8] {'panel'}, dimensions={0}, use_global_device_ids=true | all-gather | bytes 589824 | tf_op jit(solution)/shard_map/all_gather | solution.py:20
  410.2 15.0 %all_gather.85 = f32[1024,128]{0,1:T(8,128)S(1)} all-gather(f32[128,128]{0,1:T(8,128)S(1)} %fusion.19), channel_id=1, replica_groups=mesh['depth'=4,'panel'=8] {'panel'}, dimensions={0}, use_global_device_ids=true | all-gather | bytes 589824 | tf_op jit(solution)/shard_map/all_gather | solution.py:20
  425.8 1.3 collective-permute-start.6
  427.1 5.9 collective-permute-done.6
  433.0 15.1 %all_gather.86 = f32[1024,128]{0,1:T(8,128)S(1)} all-gather(f32[128,128]{0,1:T(8,128)S(1)} %collective-permute-done.6), channel_id=1, replica_groups=mesh['depth'=4,'panel'=8] {'panel'}, dimensions={0}, use_global_device_ids=true | all-gather | bytes 589824 | tf_op jit(solution)/shard_map/all_gather | solution.py:20
  448.7 15.0 %all_gather.87 = f32[1024,128]{0,1:T(8,128)S(1)} all-gather(f32[128,128]{0,1:T(8,128)S(1)} %get-tuple-element.147), channel_id=1, replica_groups=mesh['depth'=4,'panel'=8] {'panel'}, dimensions={0}, use_global_device_ids=true | all-gather | bytes 589824 | tf_op jit(solution)/shard_map/all_gather | solution.py:20
  464.3 15.0 %all_gather.88 = f32[1024,128]{0,1:T(8,128)S(1)} all-gather(f32[128,128]{0,1:T(8,128)S(1)} %fusion.12), channel_id=1, replica_groups=mesh['depth'=4,'panel'=8] {'panel'}, dimensions={0}, use_global_device_ids=true | all-gather | bytes 589824 | tf_op jit(solution)/shard_map/all_gather | solution.py:20
  481.2 5.9 collective-permute-done.7
  487.1 14.9 %all_gather.89 = f32[1024,128]{0,1:T(8,128)S(1)} all-gather(f32[128,128]{0,1:T(8,128)S(1)} %collective-permute-done.7), channel_id=1, replica_groups=mesh['depth'=4,'panel'=8] {'panel'}, dimensions={0}, use_global_device_ids=true | all-gather | bytes 589824 | tf_op jit(solution)/shard_map/all_gather | solution.py:20
  502.6 15.0 %all_gather.90 = f32[1024,128]{0,1:T(8,128)S(1)} all-gather(f32[128,128]{0,1:T(8,128)S(1)} %get-tuple-element.151), channel_id=1, replica_groups=mesh['depth'=4,'panel'=8] {'panel'}, dimensions={0}, use_global_device_ids=true | all-gather | bytes 589824 | tf_op jit(solution)/shard_map/all_gather | solution.py:20
  518.2 15.0 %all_gather.91 = f32[1024,128]{0,1:T(8,128)S(1)} all-gather(f32[128,128]{0,1:T(8,128)S(1)} %fusion.5), channel_id=1, replica_groups=mesh['depth'=4,'panel'=8] {'panel'}, dimensions={0}, use_global_device_ids=true | all-gather | bytes 589824 | tf_op jit(solution)/shard_map/all_gather | solution.py:20
  534.6 1.7 copy.25
  536.3 20.9 %all-gather.2.cloned.1.call-done = f32[1,1024,256]{1,2,0:T(8,128)} async-done(((f32[1,128,256]{1,2,0:T(8,128)}), f32[1,1024,256]{1,2,0:T(8,128)}) %all-gather.2.cloned.1.call-update) | async-done | bytes 1048592 | tf_op jit(solution)/shard_map/all_gather | solution.py:93
  557.2 66.3 %gather_fusion.1 = f32[4096]{0:T(1024)S(1)} fusion(f32[1024,256]{0,1:T(8,128)} %bitcast.382, s32[4096]{0:T(1024)S(1)} %bitcast.381), kind=kCustom, calls=%fused_computation.1 | custom fusion | bytes 65536 | tf_op jit(solution)/shard_map/jit(take_along_axis)/gather | solution.py:100
  (83 shorter events, 19.8 us)
Async XLA Ops:
  7.2 1.6 copy-start
  7.2 69.5 %reduce-scatter.5.cloned.1.call-start = ((), (), s32[]{:S(2)}) async-start(), calls=%async_computation.4 | async-start | bytes 589824 | tf_op jit(solution)/shard_map/reduce_scatter | solution.py:28
  27.2 15.5 %copy-start.1 = (f32[1,128,1024]{2,1,0:T(8,128)S(1)}, f32[1,128,1024]{2,1,0:T(8,128)}, u32[]{:S(2)}) copy-start(f32[1,128,1024]{2,1,0:T(8,128)} %param.25) | copy-start | bytes 1572868
  44.1 100.9 %reduce-scatter.7.cloned.1.call-start = ((), (), s32[]{:S(2)}) async-start(), calls=%async_computation.5 | async-start | bytes 589824 | tf_op jit(solution)/shard_map/reduce_scatter | solution.py:28
  76.7 5.5 collective-permute-start
  114.7 98.6 %reduce-scatter.9.cloned.1.call-start = ((), (), s32[]{:S(2)}) async-start(), calls=%async_computation.6 | async-start | bytes 589824 | tf_op jit(solution)/shard_map/reduce_scatter | solution.py:28
  145.1 5.6 collective-permute-start.1
  183.1 98.7 %reduce-scatter.11.cloned.1.call-start = ((), (), s32[]{:S(2)}) async-start(), calls=%async_computation.7 | async-start | bytes 589824 | tf_op jit(solution)/shard_map/reduce_scatter | solution.py:28
  213.3 5.6 collective-permute-start.2
  251.4 305.8 %all-gather.2.cloned.1.call-start = ((), (), s32[]{:S(2)}) async-start(), calls=%async_computation.8 | async-start | bytes 1179648 | tf_op jit(solution)/shard_map/all_gather | solution.py:93
  281.8 5.6 collective-permute-start.3
  318.5 6.8 %collective-permute-start.4 = (f32[128,128]{0,1:T(8,128)S(1)}, f32[128,128]{0,1:T(8,128)S(1)}, u32[]{:S(2)}, u32[]{:S(2)}) collective-permute-start(f32[128,128]{0,1:T(8,128)S(1)} %get-tuple-element.138), channel_id=1, source_target_pairs={{8,0},{16,8},{24,16},{9,1},{17,9},{25,17},{10,2},{18,10},{26,18},{... | collective-permute-start | bytes 196616 | tf_op jit(solution)/shard_map/ppermute | solution.py:15
  371.9 7.3 %collective-permute-start.5 = (f32[128,128]{0,1:T(8,128)S(1)}, f32[128,128]{0,1:T(8,128)S(1)}, u32[]{:S(2)}, u32[]{:S(2)}) collective-permute-start(f32[128,128]{0,1:T(8,128)S(1)} %get-tuple-element.142), channel_id=1, source_target_pairs={{8,0},{16,8},{24,16},{9,1},{17,9},{25,17},{10,2},{18,10},{26,18},{... | collective-permute-start | bytes 196616 | tf_op jit(solution)/shard_map/ppermute | solution.py:15
  425.8 7.2 %collective-permute-start.6 = (f32[128,128]{0,1:T(8,128)S(1)}, f32[128,128]{0,1:T(8,128)S(1)}, u32[]{:S(2)}, u32[]{:S(2)}) collective-permute-start(f32[128,128]{0,1:T(8,128)S(1)} %get-tuple-element.146), channel_id=1, source_target_pairs={{8,0},{16,8},{24,16},{9,1},{17,9},{25,17},{10,2},{18,10},{26,18},{... | collective-permute-start | bytes 196616 | tf_op jit(solution)/shard_map/ppermute | solution.py:15
  479.9 7.2 %collective-permute-start.7 = (f32[128,128]{0,1:T(8,128)S(1)}, f32[128,128]{0,1:T(8,128)S(1)}, u32[]{:S(2)}, u32[]{:S(2)}) collective-permute-start(f32[128,128]{0,1:T(8,128)S(1)} %get-tuple-element.150), channel_id=1, source_target_pairs={{8,0},{16,8},{24,16},{9,1},{17,9},{25,17},{10,2},{18,10},{26,18},{... | collective-permute-start | bytes 196616 | tf_op jit(solution)/shard_map/ppermute | solution.py:15
  518.2 16.3 %copy-start.3 = (s32[1,16]{1,0:T(1,128)S(1)}, s32[1,16]{1,0:T(1,128)}, u32[]{:S(2)}) copy-start(s32[1,16]{1,0:T(1,128)} %param.27) | copy-start | bytes 196
  533.8 0.7 copy-start.2
Sparse Core Ops, SparseCore 0:
  44.3 32.4 reduce-scatter.4
  114.8 30.1 reduce-scatter.6
  183.2 30.0 reduce-scatter.8
  251.6 30.2 reduce-scatter.10
  534.6 22.5 all-gather.1
where the time goes:
time: 633 us; the launch traced here: 631 us
  blocking collectives  331 us (52%)
  waiting for transfers between devices  175 us (28%)
  local copies, waits for them, and re-layouts  72.3 us (11%)
  starting transfers between devices  18.8 us (3%)
  matrix products  18.5 us (3%)
  between operations  14.5 us (2%)
    all_gather x22, blocking collectives, product_rows(): shard_rows = lax.all_gather(panel_rows, 'panel', axis=0, tiled=True)  331 us
    reduce_scatter x4, waiting for transfers between devices, product_transposed(): lax.psum_scatter(lax.dot_general(matrix, panel_rows, (((0,), (0,)), ((),...  122 us
    gather x2, local copies, waits for them, and re-layouts, per_device(): taken = jnp.take_along_axis(shard_rows, where_rows, axis=1)  66.3 us
    ppermute x8, waiting for transfers between devices, passed_along(): return lax.ppermute(block, axis, route)  31.8 us
    all_gather x1, waiting for transfers between devices, per_device(): shard_rows = lax.all_gather(panels, 'panel', axis=1, tiled=True)  20.9 us
    ppermute x8, starting transfers between devices, passed_along(): return lax.ppermute(block, axis, route)  18.6 us
    dot_general x22, matrix products, product_rows(): jnp.dot(columns, shard_rows, precision=highest, preferred_element_type=jn...  13 us
  transfers between devices with their start and end apart: 13, of which 13 were waited for; matrix products, arithmetic and copies ran while one was open for 0% of the time, Pallas kernels for 0%

commit v1 on v0

--- a/solution.py
+++ b/solution.py
@@ -1,6 +1,8 @@
 import jax
 import jax.numpy as jnp
 from jax import lax
+from jax.experimental import pallas as pl
+from jax.experimental.pallas import tpu as pltpu
 from jax.sharding import PartitionSpec as P
 
 ITERS = 2
@@ -48,7 +50,7 @@
     return iterate
 
 
-def per_device(diag_blocks, coupling, sources, requests):
+def per_device_general(diag_blocks, coupling, sources, requests):
     depth_count = lax.axis_size("depth")
     depth_pos = lax.axis_index("depth")
     panel_pos = lax.axis_index("panel")
@@ -102,6 +104,440 @@
     return (panels, picked)
 
 
+MESH = pl.DeviceIdType.MESH
+LEFT, RIGHT, SIBLING = 0, 1, 2
+
+
+def received(x, a, b, chips):
+    if a == x or b == x:
+        return False
+    if a == b:
+        return True
+    if a > x and b > x:
+        return a < b
+    if a < x and b < x:
+        return a > b
+    return (a < x) == (x < chips // 2)
+
+
+def split(value):
+    high = value.astype(jnp.bfloat16)
+    low = (value - high.astype(jnp.float32)).astype(jnp.bfloat16)
+    return high, low
+
+
+def sweep_kernel(
+    diag_ref, coup_ref, src_ref, req_ref,
+    out_ref, pick_ref,
+    diag_all, coup_all, diag_hi, diag_lo, coup_hi, coup_lo,
+    src_out, src_in, req_in, rhs, iterate, image, stacked, scale,
+    left_in, ahead_in, link_out, res_out, res_in, pick_out, pick_in, pick_rows,
+    d_send, d_recv, c_send, c_recv, s_send, s_recv, q_send, q_recv,
+    chain_send, chain_recv, r_send, r_recv, p_send, p_recv,
+):
+    depth_count = lax.axis_size("depth")
+    count = lax.axis_size("panel")
+    depth = lax.axis_index("depth")
+    me = lax.axis_index("panel")
+    chips = count // 2
+    chip = me // 2
+    core = lax.rem(me, 2)
+    rows = diag_ref.shape[0]
+    order = diag_ref.shape[1]
+    cols = src_out.shape[1]
+    width = order // chips
+    last = depth_count - 1
+
+    barrier = pltpu.get_barrier_semaphore()
+    for off in range(1, count):
+        pl.semaphore_signal(
+            barrier, inc=1, device_id={"panel": lax.rem(me + off, count)}, device_id_type=MESH
+        )
+
+    @pl.when(depth > 0)
+    def _():
+        pl.semaphore_signal(barrier, inc=1, device_id={"depth": depth - 1}, device_id_type=MESH)
+
+    @pl.when(depth < last)
+    def _():
+        pl.semaphore_signal(barrier, inc=1, device_id={"depth": depth + 1}, device_id_type=MESH)
+
+    src_out[...] = src_ref[...].T.reshape(count, cols, rows)
+    diag_all[me] = diag_ref[...]
+    coup_all[me] = coup_ref[...]
+
+    ends = (depth == 0).astype(jnp.int32) + (depth == last).astype(jnp.int32)
+    pl.semaphore_wait(barrier, count + 1 - ends)
+
+    neighbour = {LEFT: me - 2, RIGHT: me + 2, SIBLING: me + 1 - 2 * core}
+
+    def diag_copy(way, a, b, of_core):
+        slab = 2 * a + of_core
+        part = diag_all.at[slab, :, pl.ds(b * width, width)]
+        return pltpu.make_async_remote_copy(
+            src_ref=part, dst_ref=part,
+            send_sem=d_send.at[way, a, b], recv_sem=d_recv.at[slab, b],
+            device_id={"panel": neighbour[way]}, device_id_type=MESH,
+        )
+
+    def coup_copy(way, a, of_core):
+        slab = 2 * a + of_core
+        part = coup_all.at[slab]
+        return pltpu.make_async_remote_copy(
+            src_ref=part, dst_ref=part,
+            send_sem=c_send.at[way, a], recv_sem=c_recv.at[slab],
+            device_id={"panel": neighbour[way]}, device_id_type=MESH,
+        )
+
+    def diag_ways(x, a, b):
+        ways = []
+        if a >= x and any(received(y, a, b, chips) for y in range(x)):
+            ways.append(LEFT)
+        if a <= x and any(received(y, a, b, chips) for y in range(x + 1, chips)):
+            ways.append(RIGHT)
+        if a == x or received(x, a, b, chips):
+            ways.append(SIBLING)
+        return ways
+
+    def coup_ways(x, a):
+        ways = []
+        if a >= x and x > 0:
+            ways.append(LEFT)
+        if a <= x and x < chips - 1:
+            ways.append(RIGHT)
+        ways.append(SIBLING)
+        return ways
+
+    def arrivals(x):
+        for dist in range(1, chips):
+            for a in (x - dist, x + dist):
+                if 0 <= a < chips:
+                    yield a
+
+    def own_first(x, a):
+        return sorted(range(chips), key=lambda b: abs(b - a))
+
+    def src_copy(off):
+        to = lax.rem(me + off, count)
+        return pltpu.make_async_remote_copy(
+            src_ref=src_out.at[to], dst_ref=src_in.at[me],
+            send_sem=s_send.at[off], recv_sem=s_recv.at[off],
+            device_id={"panel": to}, device_id_type=MESH,
+        )
+
+    def req_copy(off):
+        return pltpu.make_async_remote_copy(
+            src_ref=req_ref, dst_ref=req_in.at[me],
+            send_sem=q_send.at[off], recv_sem=q_recv.at[off],
+            device_id={"panel": lax.rem(me + off, count)}, device_id_type=MESH,
+        )
+
+    for off in range(1, count):
+        src_copy(off).start()
+        req_copy(off).start()
+    src_in[me] = src_out[me]
+    req_in[me] = req_ref[...]
+
+    for x in range(chips):
+        @pl.when(chip == x)
+        def _():
+            for b in own_first(x, x):
+                for way in diag_ways(x, x, b):
+                    diag_copy(way, x, b, core).start()
+            for a in arrivals(x):
+                for b in own_first(x, a):
+                    if received(x, a, b, chips):
+                        diag_copy(SIBLING, a, b, core).wait_recv()
+                        for way in diag_ways(x, a, b):
+                            diag_copy(way, a, b, core).start()
+            for way in coup_ways(x, x):
+                coup_copy(way, x, core).start()
+            for a in range(chips):
+                for b in range(chips):
+                    if a == x or received(x, a, b, chips):
+                        diag_copy(SIBLING, a, b, 1 - core).wait_recv()
+
+    for off in range(1, count):
+        src_copy(off).wait_recv()
+        req_copy(off).wait_recv()
+
+    def expand(at, carry):
+        a, b = at // chips, lax.rem(at, chips)
+        straddle = (a < chip) != (b < chip)
+        from_left = chip < chips // 2
+        both_right = (a > chip) & (b > chip)
+        got = (a == chip) | (
+            (b != chip)
+            & (
+                (a == b)
+                | (both_right & (a < b))
+                | ((a < chip) & (b < chip) & (a > b))
+                | (straddle & ((a < chip) == from_left))
+            )
+        )
+        rows_at = pl.ds(pl.multiple_of(a * width, width), width)
+        cols_at = pl.ds(pl.multiple_of(b * width, width), width)
+
+        @pl.when(got)
+        def _():
+            high, low = split(diag_all[pl.ds(2 * a, 2), :, cols_at].reshape(width, width))
+            diag_hi[rows_at, cols_at] = high
+            diag_lo[rows_at, cols_at] = low
+
+        @pl.when(jnp.logical_not(got))
+        def _():
+            high, low = split(diag_all[pl.ds(2 * b, 2), :, rows_at].reshape(width, width).T)
+            diag_hi[rows_at, cols_at] = high
+            diag_lo[rows_at, cols_at] = low
+
+        return carry
+
+    lax.fori_loop(0, chips * chips, expand, 0)
+
+    eye = lax.broadcasted_iota(jnp.int32, (rows, rows), 0) == lax.broadcasted_iota(
+        jnp.int32, (rows, rows), 1
+    )
+    for p in range(count):
+        lanes = slice(p * rows, (p + 1) * rows)
+        scale[:, lanes] = jnp.sum(
+            jnp.where(eye, diag_all[p, :, lanes], 0.0), axis=0, keepdims=True
+        )
+        rhs[:, lanes] = src_in[p]
+
+    def widen_coup(slab):
+        high, low = split(coup_all[slab])
+        at = pl.ds(pl.multiple_of(slab * rows, rows), rows)
+        coup_hi[at, :] = high
+        coup_lo[at, :] = low
+
+    tile = width
+
+    def product(value, high_ref, low_ref, contract):
+        high, low = split(value)
+        stacked[0:cols] = high
+        stacked[cols : 2 * cols] = low
+
+        def one(n, carry):
+            at = pl.ds(pl.multiple_of(n * tile, tile), tile)
+            pick = (slice(None), at) if contract == 0 else (at, slice(None))
+            dims = (((1,), (contract,)), ((), ()))
+            both = lax.dot_general(
+                stacked[...], high_ref[pick], dims, preferred_element_type=jnp.float32
+            )
+            small = lax.dot_general(
+                stacked[0:cols], low_ref[pick], dims, preferred_element_type=jnp.float32
+            )
+            image[:, at] = both[0:cols] + (both[cols : 2 * cols] + small)
+            return carry
+
+        lax.fori_loop(0, order // tile, one, 0)
+
+    def jacobi_columns():
+        iterate[...] = rhs[...] / scale[...]
+
+        def step(sweep_no, carry):
+            product(iterate[...], diag_hi, diag_lo, 0)
+            iterate[...] = iterate[...] + (rhs[...] - image[...]) / scale[...]
+            return carry
+
+        lax.fori_loop(0, ITERS, step, 0)
+
+    @pl.when(depth == 0)
+    def _():
+        jacobi_columns()
+
+    for x in range(chips):
+        @pl.when(chip == x)
+        def _():
+            widen_coup(2 * x + core)
+            for a in arrivals(x):
+                coup_copy(SIBLING, a, core).wait_recv()
+                for way in coup_ways(x, a):
+                    coup_copy(way, a, core).start()
+                widen_coup(2 * a + core)
+    for a in range(chips):
+        coup_copy(SIBLING, a, 1 - core).wait_recv()
+        widen_coup(2 * a + 1 - core)
+
+    def chain_copy(way, to):
+        return pltpu.make_async_remote_copy(
+            src_ref=link_out.at[way], dst_ref=left_in if way == 0 else ahead_in,
+            send_sem=chain_send.at[way], recv_sem=chain_recv.at[way],
+            device_id={"depth": to}, device_id_type=MESH,
+        )
+
+    @pl.when(depth > 0)
+    def _():
+        chain_copy(0, depth).wait_recv()
+        rhs[...] = rhs[...] - left_in[...]
+
+    @pl.when((depth > 0) & (depth < last))
+    def _():
+        jacobi_columns()
+
+    @pl.when(depth < last)
+    def _():
+        product(iterate[...], coup_hi, coup_lo, 0)
+        link_out[0] = image[...]
+        chain_copy(0, depth + 1).start()
+        chain_copy(1, depth).wait_recv()
+        product(ahead_in[...], coup_hi, coup_lo, 1)
+        rhs[...] = rhs[...] - image[...]
+
+    jacobi_columns()
+
+    @pl.when(depth > 0)
+    def _():
+        link_out[1] = iterate[...]
+        chain_copy(1, depth - 1).start()
+
+    def res_copy(off):
+        to = lax.rem(me + off, count)
+        return pltpu.make_async_remote_copy(
+            src_ref=res_out.at[to], dst_ref=res_in.at[me],
+            send_sem=r_send.at[off], recv_sem=r_recv.at[off],
+            device_id={"panel": to}, device_id_type=MESH,
+        )
+
+    def pick_copy(off):
+        return pltpu.make_async_remote_copy(
+            src_ref=pick_out, dst_ref=pick_in.at[me],
+            send_sem=p_send.at[off], recv_sem=p_recv.at[off],
+            device_id={"panel": lax.rem(me + off, count)}, device_id_type=MESH,
+        )
+
+    for p in range(count):
+        res_out[p] = iterate[:, p * rows : (p + 1) * rows]
+    for off in range(1, count):
+        res_copy(off).start()
+    value = iterate[...]
+    high, low = split(value)
+    rest = ((value - high.astype(jnp.float32)) - low.astype(jnp.float32)).astype(jnp.bfloat16)
+    wanted = jnp.sum(req_in[...], axis=0)[0:1]
+    chosen = lax.broadcasted_iota(jnp.int32, (order, wanted.shape[1]), 0) == wanted
+    chosen = chosen.astype(jnp.float32).astype(jnp.bfloat16)
+
+    def take(term):
+        return jnp.dot(term, chosen, preferred_element_type=jnp.float32)
+
+    pick_out[...] = (take(rest) + take(low)) + take(high)
+    for off in range(1, count):
+        pick_copy(off).start()
+    res_in[me] = res_out[me]
+    pick_in[me] = pick_out[...]
+    for off in range(1, count):
+        res_copy(off).wait_recv()
+    out_ref[...] = res_in[...].reshape(count * cols, rows).T
+    for off in range(1, count):
+        pick_copy(off).wait_recv()
+    pick_rows[...] = pick_in[...].reshape(count * cols, pick_out.shape[1]).T
+    mine = pick_ref.shape[0]
+    pick_ref[...] = pick_rows[pl.ds(pl.multiple_of(me * mine, mine), mine), :]
+
+    for off in range(1, count):
+        src_copy(off).wait_send()
+        req_copy(off).wait_send()
+        res_copy(off).wait_send()
+        pick_copy(off).wait_send()
+
+    @pl.when(depth < last)
+    def _():
+        chain_copy(0, depth + 1).wait_send()
+
+    @pl.when(depth > 0)
+    def _():
+        chain_copy(1, depth - 1).wait_send()
+
+    for x in range(chips):
+        @pl.when(chip == x)
+        def _():
+            for a in range(chips):
+                for b in range(chips):
+                    for way in diag_ways(x, a, b):
+                        diag_copy(way, a, b, core).wait_send()
+                for way in coup_ways(x, a):
+                    coup_copy(way, a, core).wait_send()
+
+
+def per_device(diag_blocks, coupling, sources, requests):
+    count = lax.axis_size("panel")
+    block_count, rows, order = diag_blocks.shape
+    total = sources.shape[2]
+    mine = requests.shape[1]
+    if (
+        block_count != 1
+        or count % 2
+        or rows % 128
+        or order != rows * count
+        or total % (16 * count)
+        or mine % 8
+        or (mine * count) % 128
+    ):
+        return per_device_general(diag_blocks, coupling, sources, requests)
+    cols = total // count
+    chips = count // 2
+    spots = jnp.zeros((1, mine * count), jnp.int32)
+    spots = lax.dynamic_update_slice(spots, requests, (0, lax.axis_index("panel") * mine))
+    spots = jnp.broadcast_to(spots, (8, mine * count))
+    f32, half = jnp.float32, jnp.bfloat16
+    vmem = pltpu.VMEM
+    dma = pltpu.SemaphoreType.DMA
+    panels, picked = pl.pallas_call(
+        sweep_kernel,
+        out_shape=(
+            jax.ShapeDtypeStruct((rows, total), f32),
+            jax.ShapeDtypeStruct((mine, total), f32),
+        ),
+        in_specs=[pl.BlockSpec(memory_space=vmem)] * 4,
+        out_specs=(pl.BlockSpec(memory_space=vmem), pl.BlockSpec(memory_space=vmem)),
+        scratch_shapes=[
+            vmem((count, rows, order), f32),
+            vmem((count, rows, order), f32),
+            vmem((order, order), half),
+            vmem((order, order), half),
+            vmem((order, order), half),
+            vmem((order, order), half),
+            vmem((count, cols, rows), f32),
+            vmem((count, cols, rows), f32),
+            vmem((count, 8, mine * count), jnp.int32),
+            vmem((cols, order), f32),
+            vmem((cols, order), f32),
+            vmem((cols, order), f32),
+            vmem((2 * cols, order), half),
+            vmem((1, order), f32),
+            vmem((cols, order), f32),
+            vmem((cols, order), f32),
+            vmem((2, cols, order), f32),
+            vmem((count, cols, rows), f32),
+            vmem((count, cols, rows), f32),
+            vmem((cols, mine * count), f32),
+            vmem((count, cols, mine * count), f32),
+            vmem((mine * count, total), f32),
+            dma((3, chips, chips)),
+            dma((count, chips)),
+            dma((3, chips)),
+            dma((count,)),
+            dma((count,)),
+            dma((count,)),
+            dma((count,)),
+            dma((count,)),
+            dma((2,)),
+            dma((2,)),
+            dma((count,)),
+            dma((count,)),
+            dma((count,)),
+            dma((count,)),
+        ],
+        compiler_params=pltpu.CompilerParams(
+            collective_id=0, has_side_effects=True, vmem_limit_bytes=48 * 2**20
+        ),
+        cost_estimate=pl.CostEstimate(
+            flops=36 * order * order * cols, bytes_accessed=16 * rows * order, transcendentals=0
+        ),
+    )(diag_blocks[0], coupling[0], sources[0], spots)
+    return panels[None], picked[None]
+
+
 def solution(mesh):
     placed = (
         P("depth", "panel", None),

time: 633 us -> 125 us (0.20)
  blocking collectives: 331 us -> 0 us
  waiting for transfers between devices: 175 us -> 0 us
  Pallas kernels: 0 us -> 119 us
  local copies, waits for them, and re-layouts: 72.3 us -> 4.98 us
  starting transfers between devices: 18.8 us -> 0 us
  matrix products: 18.5 us -> 0 us
  between operations: 14.5 us -> 0.66 us
    all_gather x22 -> x0, blocking collectives: 331 us -> none  [product_rows(): shard_rows = lax.all_gather(panel_rows, 'panel', axis=0, tiled=True)]
    reduce_scatter x4 -> x0, waiting for transfers between devices: 122 us -> none  [product_transposed(): lax.psum_scatter(lax.dot_general(matrix, panel_rows, (((0,), (0,)), ((),...]
    pallas_call x0 -> x1, Pallas kernels: none -> 119 us  [per_device(): pl.pallas_call(sweep_kernel, out_shape=(jax.ShapeDtypeStruct((rows, total...]
    gather x3 -> x0, local copies, waits for them, and re-layouts: 67.6 us -> none  [the longest x2 66.3 us: per_device(): taken = jnp.take_along_axis(shard_rows, where_rows, axis=1)]
    ppermute x8 -> x0, waiting for transfers between devices: 31.8 us -> none  [passed_along(): return lax.ppermute(block, axis, route)]
    all_gather x1 -> x0, waiting for transfers between devices: 20.9 us -> none  [per_device(): shard_rows = lax.all_gather(panels, 'panel', axis=1, tiled=True)]
    ppermute x8 -> x0, starting transfers between devices: 18.6 us -> none  [passed_along(): return lax.ppermute(block, axis, route)]
    dot_general x26 -> x0, matrix products: 18.5 us -> none  [the longest x22 13 us: product_rows(): jnp.dot(columns, shard_rows, precision=highest, preferred_element_type=jn...]
  transfers between devices with their start and end apart: 13 -> 0, of which waited for: 13 -> 0; matrix products, arithmetic and copies ran while one was open for 0% -> 0% of each run, Pallas kernels for 0% -> 0%
where the time goes in v1:
time: 125 us; the launch traced here: 124 us
  Pallas kernels  119 us (95%)
  local copies, waits for them, and re-layouts  4.98 us (4%)
    pallas_call x1, Pallas kernels, per_device(): pl.pallas_call(sweep_kernel, out_shape=(jax.ShapeDtypeStruct((rows, total...  119 us
    unnamed x10, local copies, waits for them, and re-layouts  4.89 us

profile of v1, /device:TPU:0, one launch (start us, length us, event | category | flops | bytes accessed | tf_op | source)
XLA Modules:
  0.0 124.3 jit_solution(12532253371067125342)
XLA Ops:
  0.6 0.0 copy-start.3
  0.7 0.6 copy-done.3
  1.3 0.1 bitcast_dynamic-update-slice_fusion
  1.4 0.0 copy-start
  1.4 1.0 copy-done
  2.4 0.0 copy-start.1
  2.4 1.0 copy-done.1
  3.5 0.0 copy-start.2
  3.5 0.9 copy-done.2
  4.4 118.6 %shard_map.59 = (f32[128,256]{1,0:T(8,128)S(1)}, f32[16,256]{1,0:T(8,128)S(1)}) custom-call(f32[128,1024]{1,0:T(8,128)S(1)} %bitcast.9, f32[128,1024]{1,0:T(8,128)S(1)} %bitcast.10, f32[128,256]{1,0:T(8,128)S(1)} %bitcast.11, s32[8,128]{1,0:T(8,128)S(1)} %broadcast_in_dim.18.req_ref), custom_call_target="tpu_custom_call" | custom-call | flops 1207959552 | bytes 2097152 | tf_op jit(solution)/shard_map/pallas_call | solution.py:485
  123.0 0.7 copy.9
  123.7 0.6 copy.10
  (2 shorter events, 0.0 us)
Async XLA Ops:
  0.6 0.7 copy-start.3
  1.4 1.0 copy-start
  2.4 1.0 copy-start.1
  3.5 0.9 copy-start.2

commit v2 on v1

--- a/solution.py
+++ b/solution.py
@@ -129,8 +129,8 @@
 def sweep_kernel(
     diag_ref, coup_ref, src_ref, req_ref,
     out_ref, pick_ref,
-    diag_all, coup_all, diag_hi, diag_lo, coup_hi, coup_lo,
-    src_out, src_in, req_in, rhs, iterate, image, stacked, scale,
+    diag_all, coup_all, diag_hi, diag_lo, map_hi, map_lo, edge_hi, edge_lo, part_hi, part_lo, edge,
+    src_out, src_in, req_in, rhs, iterate, forward, stacked, scale, scale_col, factors,
     left_in, ahead_in, link_out, res_out, res_in, pick_out, pick_in, pick_rows,
     d_send, d_recv, c_send, c_recv, s_send, s_recv, q_send, q_recv,
     chain_send, chain_recv, r_send, r_recv, p_send, p_recv,
@@ -199,15 +199,6 @@
             ways.append(SIBLING)
         return ways
 
-    def coup_ways(x, a):
-        ways = []
-        if a >= x and x > 0:
-            ways.append(LEFT)
-        if a <= x and x < chips - 1:
-            ways.append(RIGHT)
-        ways.append(SIBLING)
-        return ways
-
     def arrivals(x):
         for dist in range(1, chips):
             for a in (x - dist, x + dist):
@@ -250,12 +241,25 @@
                         diag_copy(SIBLING, a, b, core).wait_recv()
                         for way in diag_ways(x, a, b):
                             diag_copy(way, a, b, core).start()
-            for way in coup_ways(x, x):
-                coup_copy(way, x, core).start()
             for a in range(chips):
                 for b in range(chips):
                     if a == x or received(x, a, b, chips):
                         diag_copy(SIBLING, a, b, 1 - core).wait_recv()
+
+    def coup_each(a, act):
+        @pl.when((a >= chip) & (chip > 0))
+        def _():
+            act(coup_copy(LEFT, a, core))
+
+        @pl.when((a <= chip) & (chip < chips - 1))
+        def _():
+            act(coup_copy(RIGHT, a, core))
+
+        act(coup_copy(SIBLING, a, core))
+
+    @pl.when(depth < last)
+    def _():
+        coup_each(chip, lambda copy: copy.start())
 
     for off in range(1, count):
         src_copy(off).wait_recv()
@@ -302,17 +306,121 @@
         scale[:, lanes] = jnp.sum(
             jnp.where(eye, diag_all[p, :, lanes], 0.0), axis=0, keepdims=True
         )
+        scale_col[lanes, :] = jnp.sum(
+            jnp.where(eye, diag_all[p, :, lanes], 0.0), axis=1, keepdims=True
+        )
         rhs[:, lanes] = src_in[p]
 
-    def widen_coup(slab):
-        high, low = split(coup_all[slab])
-        at = pl.ds(pl.multiple_of(slab * rows, rows), rows)
-        coup_hi[at, :] = high
-        coup_lo[at, :] = low
-
     tile = width
-
-    def product(value, high_ref, low_ref, contract):
+    tall = 2 * width
+    tiny = 1.0 / order
+
+    def sums(n, carry):
+        at = pl.ds(pl.multiple_of(n * tile, tile), tile)
+        total = jnp.sum(jnp.abs(diag_hi[:, at].astype(jnp.float32)) * tiny, axis=0, keepdims=True)
+        return jnp.maximum(carry, total / scale[:, at])
+
+    largest = lax.fori_loop(0, chips, sums, jnp.zeros((1, tile), jnp.float32))
+    largest = jnp.max(largest, axis=1, keepdims=True) * (1.02 * order)
+    largest = jnp.maximum(largest, 1.0)
+    least = jnp.min(scale[...], axis=1, keepdims=True)
+    factors[0:1] = jnp.broadcast_to(largest, (1, tile))
+    factors[1:2] = jnp.broadcast_to(least, (1, tile))
+
+    def identity(i, n):
+        down = lax.broadcasted_iota(jnp.int32, (tile, tile), 0) + i * tile
+        over = lax.broadcasted_iota(jnp.int32, (tile, tile), 1) + n * tile
+        return down == over
+
+    def over_diag(value, rows_at):
+        part = scale_col[rows_at, :]
+        ease = jnp.where(part > 1.0, 2.0**-30, 1.0)
+        return (value * ease) * (1.0 / (part * ease))
+
+    def across(at):
+        return factors[1:2] / scale[:, at] / factors[0:1] / factors[0:1]
+
+    def first_step(at_tile, carry):
+        i, n = at_tile // chips, lax.rem(at_tile, chips)
+        rows_at = pl.ds(pl.multiple_of(i * tile, tile), tile)
+        at = pl.ds(pl.multiple_of(n * tile, tile), tile)
+        ratio = diag_hi[rows_at, at].astype(jnp.float32) + diag_lo[rows_at, at].astype(jnp.float32)
+        ratio = over_diag(ratio, rows_at)
+        high, low = split((jnp.where(identity(i, n), 2.0, 0.0) - ratio) * across(at))
+        edge_hi[rows_at, at] = high
+        edge_lo[rows_at, at] = low
+        return carry
+
+    lax.fori_loop(0, chips * chips, first_step, 0)
+
+    def dot(left, right, contract=0):
+        return lax.dot_general(
+            left, right, (((1,), (contract,)), ((), ())), preferred_element_type=jnp.float32
+        )
+
+    def second_step(at_tile, carry):
+        i, n = at_tile // chips, lax.rem(at_tile, chips)
+        rows_at = pl.ds(pl.multiple_of(i * tile, tile), tile)
+        at = pl.ds(pl.multiple_of(n * tile, tile), tile)
+        moved = dot(diag_hi[rows_at, :], edge_hi[:, at]) + (
+            dot(diag_hi[rows_at, :], edge_lo[:, at]) + dot(diag_lo[rows_at, :], edge_hi[:, at])
+        )
+        start = edge_hi[rows_at, at].astype(jnp.float32) + edge_lo[rows_at, at].astype(jnp.float32)
+        moved = jnp.where(identity(i, n), across(at), 0.0) - over_diag(moved, rows_at)
+        high, low = split(start + moved)
+        map_hi[rows_at, at] = high
+        map_lo[rows_at, at] = low
+        return carry
+
+    lax.fori_loop(0, chips * chips, second_step, 0)
+
+    def add_slab(a, first):
+        high, low = split(coup_all[pl.ds(2 * a, 2)].reshape(width, order))
+        part_hi[...] = high
+        part_lo[...] = low
+        along = pl.ds(pl.multiple_of(a * width, width), width)
+
+        def one(at_tile, carry):
+            i, n = lax.rem(at_tile, order // tall), at_tile // (order // tall)
+            rows_at = pl.ds(pl.multiple_of(i * tall, tall), tall)
+            at = pl.ds(pl.multiple_of(n * tile, tile), tile)
+            term = dot(map_hi[rows_at, along], part_hi[:, at]) + (
+                dot(map_hi[rows_at, along], part_lo[:, at])
+                + dot(map_lo[rows_at, along], part_hi[:, at])
+            )
+            edge[rows_at, at] = term if first else edge[rows_at, at] + term
+            return carry
+
+        lax.fori_loop(0, (order // tall) * chips, one, 0)
+
+    @pl.when(depth < last)
+    def _():
+        coup_copy(SIBLING, chip, 1 - core).wait_recv()
+        add_slab(chip, True)
+        for dist in range(1, chips):
+            sides = [(chip - dist, chip - dist >= 0), (chip + dist, chip + dist < chips)]
+            for a, there in sides:
+                @pl.when(there)
+                def _():
+                    coup_copy(SIBLING, a, core).wait_recv()
+                    coup_each(a, lambda copy: copy.start())
+
+            for a, there in sides:
+                @pl.when(there)
+                def _():
+                    coup_copy(SIBLING, a, 1 - core).wait_recv()
+                    add_slab(a, False)
+
+        def narrow(i, carry):
+            rows_at = pl.ds(pl.multiple_of(i * tile, tile), tile)
+            high, low = split(edge[rows_at, :])
+            edge_hi[rows_at, :] = high
+            edge_lo[rows_at, :] = low
+            return carry
+
+        lax.fori_loop(0, chips, narrow, 0)
+
+    def product(value, high_ref, low_ref, contract, finish):
         high, low = split(value)
         stacked[0:cols] = high
         stacked[cols : 2 * cols] = low
@@ -320,76 +428,58 @@
         def one(n, carry):
             at = pl.ds(pl.multiple_of(n * tile, tile), tile)
             pick = (slice(None), at) if contract == 0 else (at, slice(None))
-            dims = (((1,), (contract,)), ((), ()))
-            both = lax.dot_general(
-                stacked[...], high_ref[pick], dims, preferred_element_type=jnp.float32
-            )
-            small = lax.dot_general(
-                stacked[0:cols], low_ref[pick], dims, preferred_element_type=jnp.float32
-            )
-            image[:, at] = both[0:cols] + (both[cols : 2 * cols] + small)
+            both = dot(stacked[...], high_ref[pick], contract)
+            small = dot(stacked[0:cols], low_ref[pick], contract)
+            image = both[0:cols] + (both[cols : 2 * cols] + small)
+            finish(n, at, image * factors[0:1] / factors[1:2] * factors[0:1])
             return carry
 
-        lax.fori_loop(0, order // tile, one, 0)
-
-    def jacobi_columns():
-        iterate[...] = rhs[...] / scale[...]
-
-        def step(sweep_no, carry):
-            product(iterate[...], diag_hi, diag_lo, 0)
-            iterate[...] = iterate[...] + (rhs[...] - image[...]) / scale[...]
-            return carry
-
-        lax.fori_loop(0, ITERS, step, 0)
-
-    @pl.when(depth == 0)
-    def _():
-        jacobi_columns()
-
-    for x in range(chips):
-        @pl.when(chip == x)
+        lax.fori_loop(0, chips, one, 0)
+
+    def chain_copy(way, n, to):
+        at = pl.ds(pl.multiple_of(n * tile, tile), tile)
+        into = left_in if way == 0 else ahead_in
+        return pltpu.make_async_remote_copy(
+            src_ref=link_out.at[way, :, at], dst_ref=into.at[:, at],
+            send_sem=chain_send.at[way, n], recv_sem=chain_recv.at[way, n],
+            device_id={"depth": to}, device_id_type=MESH,
+        )
+
+    def send_left(n, at, image):
+        link_out[0, :, at] = image
+        chain_copy(0, n, depth + 1).start()
+
+    def keep_forward(n, at, image):
+        forward[:, at] = image
+
+    def send_panel(n, at, image):
+        iterate[:, at] = image
+
+        @pl.when(depth > 0)
         def _():
-            widen_coup(2 * x + core)
-            for a in arrivals(x):
-                coup_copy(SIBLING, a, core).wait_recv()
-                for way in coup_ways(x, a):
-                    coup_copy(way, a, core).start()
-                widen_coup(2 * a + core)
-    for a in range(chips):
-        coup_copy(SIBLING, a, 1 - core).wait_recv()
-        widen_coup(2 * a + 1 - core)
-
-    def chain_copy(way, to):
-        return pltpu.make_async_remote_copy(
-            src_ref=link_out.at[way], dst_ref=left_in if way == 0 else ahead_in,
-            send_sem=chain_send.at[way], recv_sem=chain_recv.at[way],
-            device_id={"depth": to}, device_id_type=MESH,
-        )
+            link_out[1, :, at] = image
+            chain_copy(1, n, depth - 1).start()
 
     @pl.when(depth > 0)
     def _():
-        chain_copy(0, depth).wait_recv()
+        for n in range(chips):
+            chain_copy(0, n, depth).wait_recv()
         rhs[...] = rhs[...] - left_in[...]
 
-    @pl.when((depth > 0) & (depth < last))
-    def _():
-        jacobi_columns()
-
     @pl.when(depth < last)
     def _():
-        product(iterate[...], coup_hi, coup_lo, 0)
-        link_out[0] = image[...]
-        chain_copy(0, depth + 1).start()
-        chain_copy(1, depth).wait_recv()
-        product(ahead_in[...], coup_hi, coup_lo, 1)
-        rhs[...] = rhs[...] - image[...]
-
-    jacobi_columns()
-
-    @pl.when(depth > 0)
-    def _():
-        link_out[1] = iterate[...]
-        chain_copy(1, depth - 1).start()
+        product(rhs[...], edge_hi, edge_lo, 0, send_left)
+        product(rhs[...], map_hi, map_lo, 0, keep_forward)
+        for n in range(chips):
+            chain_copy(1, n, depth).wait_recv()
+        product(
+            ahead_in[...], edge_hi, edge_lo, 1,
+            lambda n, at, image: send_panel(n, at, forward[:, at] - image),
+        )
+
+    @pl.when(depth == last)
+    def _():
+        product(rhs[...], map_hi, map_lo, 0, send_panel)
 
     def res_copy(off):
         to = lax.rem(me + off, count)
@@ -442,11 +532,15 @@
 
     @pl.when(depth < last)
     def _():
-        chain_copy(0, depth + 1).wait_send()
+        for n in range(chips):
+            chain_copy(0, n, depth + 1).wait_send()
+        for a in range(chips):
+            coup_each(a, lambda copy: copy.wait_send())
 
     @pl.when(depth > 0)
     def _():
-        chain_copy(1, depth - 1).wait_send()
+        for n in range(chips):
+            chain_copy(1, n, depth - 1).wait_send()
 
     for x in range(chips):
         @pl.when(chip == x)
@@ -455,8 +549,6 @@
                 for b in range(chips):
                     for way in diag_ways(x, a, b):
                         diag_copy(way, a, b, core).wait_send()
-                for way in coup_ways(x, a):
-                    coup_copy(way, a, core).wait_send()
 
 
 def per_device(diag_blocks, coupling, sources, requests):
@@ -497,6 +589,11 @@
             vmem((order, order), half),
             vmem((order, order), half),
             vmem((order, order), half),
+            vmem((order, order), half),
+            vmem((order, order), half),
+            vmem((2 * rows, order), half),
+            vmem((2 * rows, order), half),
+            vmem((order, order), f32),
             vmem((count, cols, rows), f32),
             vmem((count, cols, rows), f32),
             vmem((count, 8, mine * count), jnp.int32),
@@ -505,6 +602,8 @@
             vmem((cols, order), f32),
             vmem((2 * cols, order), half),
             vmem((1, order), f32),
+            vmem((order, 1), f32),
+            vmem((2, 2 * rows), f32),
             vmem((cols, order), f32),
             vmem((cols, order), f32),
             vmem((2, cols, order), f32),
@@ -521,8 +620,8 @@
             dma((count,)),
             dma((count,)),
             dma((count,)),
-            dma((2,)),
-            dma((2,)),
+            dma((2, chips)),
+            dma((2, chips)),
             dma((count,)),
             dma((count,)),
             dma((count,)),

time: 125 us -> 118 us (0.944)
  Pallas kernels: 119 us -> 112 us
    pallas_call x1, Pallas kernels: 119 us -> 112 us  [per_device(): pl.pallas_call(sweep_kernel, out_shape=(jax.ShapeDtypeStruct((rows, total...]
where the time goes in v2:
time: 118 us
  Pallas kernels  112 us (95%)
  local copies, waits for them, and re-layouts  4.98 us (4%)
    pallas_call x1, Pallas kernels, per_device(): pl.pallas_call(sweep_kernel, out_shape=(jax.ShapeDtypeStruct((rows, total...  112 us
    unnamed x10, local copies, waits for them, and re-layouts  4.89 us

profile of v2, /device:TPU:0, one launch (start us, length us, event | category | flops | bytes accessed | tf_op | source)
XLA Modules:
  0.0 117.8 jit_solution(3472383876662980896)
XLA Ops:
  0.6 0.0 copy-start.3
  0.7 0.6 copy-done.3
  1.3 0.1 bitcast_dynamic-update-slice_fusion
  1.4 0.0 copy-start
  1.4 1.0 copy-done
  2.4 0.0 copy-start.1
  2.4 1.0 copy-done.1
  3.5 0.0 copy-start.2
  3.5 0.9 copy-done.2
  4.4 112.1 %shard_map.59 = (f32[128,256]{1,0:T(8,128)S(1)}, f32[16,256]{1,0:T(8,128)S(1)}) custom-call(f32[128,1024]{1,0:T(8,128)S(1)} %bitcast.9, f32[128,1024]{1,0:T(8,128)S(1)} %bitcast.10, f32[128,256]{1,0:T(8,128)S(1)} %bitcast.11, s32[8,128]{1,0:T(8,128)S(1)} %broadcast_in_dim.18.req_ref), custom_call_target="tpu_custom_call" | custom-call | flops 1207959552 | bytes 2097152 | tf_op jit(solution)/shard_map/pallas_call | solution.py:577
  116.5 0.7 copy.9
  117.2 0.6 copy.10
  (2 shorter events, 0.0 us)
Async XLA Ops:
  0.6 0.7 copy-start.3
  1.4 1.0 copy-start
  2.4 1.0 copy-start.1
  3.5 0.9 copy-start.2

commit v3 on v2

--- a/solution.py
+++ b/solution.py
@@ -130,9 +130,9 @@
     diag_ref, coup_ref, src_ref, req_ref,
     out_ref, pick_ref,
     diag_all, coup_all, diag_hi, diag_lo, map_hi, map_lo, edge_hi, edge_lo, part_hi, part_lo, edge,
-    src_out, src_in, req_in, rhs, iterate, forward, stacked, scale, scale_col, factors,
+    src_out, src_in, req_in, rhs, iterate, forward, stacked, total, src_own, scale, scale_col, factors,
     left_in, ahead_in, link_out, res_out, res_in, pick_out, pick_in, pick_rows,
-    d_send, d_recv, c_send, c_recv, s_send, s_recv, q_send, q_recv,
+    load, d_send, d_recv, c_send, c_recv, s_send, s_recv, q_send, q_recv,
     chain_send, chain_recv, r_send, r_recv, p_send, p_recv,
 ):
     depth_count = lax.axis_size("depth")
@@ -148,6 +148,13 @@
     width = order // chips
     last = depth_count - 1
 
+    loads = [
+        pltpu.make_async_copy(src_ref, src_own, load.at[0]),
+        pltpu.make_async_copy(diag_ref, diag_all.at[me], load.at[1]),
+        pltpu.make_async_copy(coup_ref, coup_all.at[me], load.at[2]),
+    ]
+    for copy in loads:
+        copy.start()
     barrier = pltpu.get_barrier_semaphore()
     for off in range(1, count):
         pl.semaphore_signal(
@@ -162,9 +169,10 @@
     def _():
         pl.semaphore_signal(barrier, inc=1, device_id={"depth": depth + 1}, device_id_type=MESH)
 
-    src_out[...] = src_ref[...].T.reshape(count, cols, rows)
-    diag_all[me] = diag_ref[...]
-    coup_all[me] = coup_ref[...]
+    loads[0].wait()
+    src_out[...] = src_own[...].T.reshape(count, cols, rows)
+    loads[1].wait()
+    loads[2].wait()
 
     ends = (depth == 0).astype(jnp.int32) + (depth == last).astype(jnp.int32)
     pl.semaphore_wait(barrier, count + 1 - ends)
@@ -229,6 +237,22 @@
     src_in[me] = src_out[me]
     req_in[me] = req_ref[...]
 
+    def coup_each(a, act):
+        @pl.when((a >= chip) & (chip > 0))
+        def _():
+            act(coup_copy(LEFT, a, core))
+
+        @pl.when((a <= chip) & (chip < chips - 1))
+        def _():
+            act(coup_copy(RIGHT, a, core))
+
+        act(coup_copy(SIBLING, a, core))
+
+    def coup_first():
+        @pl.when(depth < last)
+        def _():
+            coup_each(chip, lambda copy: copy.start())
+
     for x in range(chips):
         @pl.when(chip == x)
         def _():
@@ -241,25 +265,17 @@
                         diag_copy(SIBLING, a, b, core).wait_recv()
                         for way in diag_ways(x, a, b):
                             diag_copy(way, a, b, core).start()
+                if x in (0, chips - 1) and abs(a - x) == 1:
+                    for b in range(chips):
+                        for way in diag_ways(x, x, b):
+                            diag_copy(way, x, b, core).wait_send()
+                    coup_first()
+            if x not in (0, chips - 1):
+                coup_first()
             for a in range(chips):
                 for b in range(chips):
                     if a == x or received(x, a, b, chips):
                         diag_copy(SIBLING, a, b, 1 - core).wait_recv()
-
-    def coup_each(a, act):
-        @pl.when((a >= chip) & (chip > 0))
-        def _():
-            act(coup_copy(LEFT, a, core))
-
-        @pl.when((a <= chip) & (chip < chips - 1))
-        def _():
-            act(coup_copy(RIGHT, a, core))
-
-        act(coup_copy(SIBLING, a, core))
-
-    @pl.when(depth < last)
-    def _():
-        coup_each(chip, lambda copy: copy.start())
 
     for off in range(1, count):
         src_copy(off).wait_recv()
@@ -372,9 +388,27 @@
         map_lo[rows_at, at] = low
         return carry
 
-    lax.fori_loop(0, chips * chips, second_step, 0)
-
-    def add_slab(a, first):
+    def sides(dist):
+        return [(chip - dist, chip - dist >= 0), (chip + dist, chip + dist < chips)]
+
+    def pass_on(dist):
+        for a, there in sides(dist):
+            @pl.when(there)
+            def _():
+                coup_copy(SIBLING, a, core).wait_recv()
+                coup_each(a, lambda copy: copy.start())
+
+    at_end = (chip == 0) | (chip == chips - 1)
+    sending = depth < last
+    lax.fori_loop(0, chips * chips // 2, second_step, 0)
+
+    @pl.when(sending & jnp.logical_not(at_end))
+    def _():
+        pass_on(1)
+
+    lax.fori_loop(chips * chips // 2, chips * chips, second_step, 0)
+
+    def add_slab(a, first, final=False):
         high, low = split(coup_all[pl.ds(2 * a, 2)].reshape(width, order))
         part_hi[...] = high
         part_lo[...] = low
@@ -388,24 +422,28 @@
                 dot(map_hi[rows_at, along], part_lo[:, at])
                 + dot(map_lo[rows_at, along], part_hi[:, at])
             )
-            edge[rows_at, at] = term if first else edge[rows_at, at] + term
+            term = term if first else edge[rows_at, at] + term
+            if final:
+                high, low = split(term)
+                edge_hi[rows_at, at] = high
+                edge_lo[rows_at, at] = low
+            else:
+                edge[rows_at, at] = term
             return carry
 
         lax.fori_loop(0, (order // tall) * chips, one, 0)
 
-    @pl.when(depth < last)
+    @pl.when(sending)
     def _():
         coup_copy(SIBLING, chip, 1 - core).wait_recv()
         add_slab(chip, True)
-        for dist in range(1, chips):
-            sides = [(chip - dist, chip - dist >= 0), (chip + dist, chip + dist < chips)]
-            for a, there in sides:
-                @pl.when(there)
-                def _():
-                    coup_copy(SIBLING, a, core).wait_recv()
-                    coup_each(a, lambda copy: copy.start())
-
-            for a, there in sides:
+
+    @pl.when(sending & jnp.logical_not(at_end))
+    def _():
+        for dist in range(1, chips - 1):
+            if dist + 1 < chips - 1:
+                pass_on(dist + 1)
+            for a, there in sides(dist):
                 @pl.when(there)
                 def _():
                     coup_copy(SIBLING, a, 1 - core).wait_recv()
@@ -420,21 +458,39 @@
 
         lax.fori_loop(0, chips, narrow, 0)
 
-    def product(value, high_ref, low_ref, contract, finish):
-        high, low = split(value)
-        stacked[0:cols] = high
-        stacked[cols : 2 * cols] = low
-
-        def one(n, carry):
-            at = pl.ds(pl.multiple_of(n * tile, tile), tile)
-            pick = (slice(None), at) if contract == 0 else (at, slice(None))
-            both = dot(stacked[...], high_ref[pick], contract)
-            small = dot(stacked[0:cols], low_ref[pick], contract)
-            image = both[0:cols] + (both[cols : 2 * cols] + small)
-            finish(n, at, image * factors[0:1] / factors[1:2] * factors[0:1])
-            return carry
-
-        lax.fori_loop(0, chips, one, 0)
+    @pl.when(sending & at_end)
+    def _():
+        for dist in range(1, chips):
+            pass_on(dist)
+            a = jnp.where(chip == 0, dist, chip - dist)
+            coup_copy(SIBLING, a, 1 - core).wait_recv()
+            add_slab(a, False, dist == chips - 1)
+
+    def product(part, high_ref, low_ref, contract, finish):
+        for k in range(chips):
+            lanes = slice(k * tile, (k + 1) * tile)
+            high, low = split(part(k, lanes))
+            stacked[0:cols] = high
+            stacked[cols : 2 * cols] = low
+
+            def term(at):
+                pick = (lanes, at) if contract == 0 else (at, lanes)
+                both = dot(stacked[...], high_ref[pick], contract)
+                small = dot(stacked[0:cols], low_ref[pick], contract)
+                return both[0:cols] + (both[cols : 2 * cols] + small)
+
+            def add(n, carry):
+                at = pl.ds(pl.multiple_of(n * tile, tile), tile)
+                total[:, at] = term(at) if k == 0 else total[:, at] + term(at)
+                return carry
+
+            def end(n, carry):
+                at = pl.ds(pl.multiple_of(n * tile, tile), tile)
+                image = total[:, at] + term(at)
+                finish(n, at, image * factors[0:1] / factors[1:2] * factors[0:1])
+                return carry
+
+            lax.fori_loop(0, chips, add if k < chips - 1 else end, 0, unroll=k < chips - 1)
 
     def chain_copy(way, n, to):
         at = pl.ds(pl.multiple_of(n * tile, tile), tile)
@@ -460,26 +516,30 @@
             link_out[1, :, at] = image
             chain_copy(1, n, depth - 1).start()
 
-    @pl.when(depth > 0)
-    def _():
-        for n in range(chips):
-            chain_copy(0, n, depth).wait_recv()
-        rhs[...] = rhs[...] - left_in[...]
+    def rest_part(k, lanes):
+        @pl.when(depth > 0)
+        def _():
+            chain_copy(0, k, depth).wait_recv()
+            rhs[:, lanes] = rhs[:, lanes] - left_in[:, lanes]
+
+        return rhs[:, lanes]
+
+    def ahead_part(k, lanes):
+        chain_copy(1, k, depth).wait_recv()
+        return ahead_in[:, lanes]
 
     @pl.when(depth < last)
     def _():
-        product(rhs[...], edge_hi, edge_lo, 0, send_left)
-        product(rhs[...], map_hi, map_lo, 0, keep_forward)
-        for n in range(chips):
-            chain_copy(1, n, depth).wait_recv()
+        product(rest_part, edge_hi, edge_lo, 0, send_left)
+        product(lambda k, lanes: rhs[:, lanes], map_hi, map_lo, 0, keep_forward)
         product(
-            ahead_in[...], edge_hi, edge_lo, 1,
+            ahead_part, edge_hi, edge_lo, 1,
             lambda n, at, image: send_panel(n, at, forward[:, at] - image),
         )
 
     @pl.when(depth == last)
     def _():
-        product(rhs[...], map_hi, map_lo, 0, send_panel)
+        product(rest_part, map_hi, map_lo, 0, send_panel)
 
     def res_copy(off):
         to = lax.rem(me + off, count)
@@ -548,7 +608,8 @@
             for a in range(chips):
                 for b in range(chips):
                     for way in diag_ways(x, a, b):
-                        diag_copy(way, a, b, core).wait_send()
+                        if x not in (0, chips - 1) or a != x:
+                            diag_copy(way, a, b, core).wait_send()
 
 
 def per_device(diag_blocks, coupling, sources, requests):
@@ -559,6 +620,7 @@
     if (
         block_count != 1
         or count % 2
+        or count < 4
         or rows % 128
         or order != rows * count
         or total % (16 * count)
@@ -580,7 +642,7 @@
             jax.ShapeDtypeStruct((rows, total), f32),
             jax.ShapeDtypeStruct((mine, total), f32),
         ),
-        in_specs=[pl.BlockSpec(memory_space=vmem)] * 4,
+        in_specs=[pl.BlockSpec(memory_space=pl.ANY)] * 3 + [pl.BlockSpec(memory_space=vmem)],
         out_specs=(pl.BlockSpec(memory_space=vmem), pl.BlockSpec(memory_space=vmem)),
         scratch_shapes=[
             vmem((count, rows, order), f32),
@@ -600,7 +662,9 @@
             vmem((cols, order), f32),
             vmem((cols, order), f32),
             vmem((cols, order), f32),
-            vmem((2 * cols, order), half),
+            vmem((2 * cols, 2 * rows), half),
+            vmem((cols, order), f32),
+            vmem((rows, total), f32),
             vmem((1, order), f32),
             vmem((order, 1), f32),
             vmem((2, 2 * rows), f32),
@@ -612,6 +676,7 @@
             vmem((cols, mine * count), f32),
             vmem((count, cols, mine * count), f32),
             vmem((mine * count, total), f32),
+            dma((3,)),
             dma((3, chips, chips)),
             dma((count, chips)),
             dma((3, chips)),

time: 118 us -> 107 us (0.907)
  Pallas kernels: 112 us -> 101 us
    pallas_call x1, Pallas kernels: 112 us -> 101 us  [per_device(): pl.pallas_call(sweep_kernel, out_shape=(jax.ShapeDtypeStruct((rows, total...]
where the time goes in v3:
time: 107 us
  Pallas kernels  101 us (94%)
  local copies, waits for them, and re-layouts  4.98 us (5%)
    pallas_call x1, Pallas kernels, per_device(): pl.pallas_call(sweep_kernel, out_shape=(jax.ShapeDtypeStruct((rows, total...  101 us
    unnamed x10, local copies, waits for them, and re-layouts  4.89 us

profile of v3, /device:TPU:0, one launch (start us, length us, event | category | flops | bytes accessed | tf_op | source)
XLA Modules:
  0.0 106.7 jit_solution(6857357245758951132)
XLA Ops:
  0.6 0.0 copy-start.3
  0.7 0.6 copy-done.3
  1.3 0.1 bitcast_dynamic-update-slice_fusion
  1.4 0.0 copy-start
  1.4 1.0 copy-done
  2.4 0.0 copy-start.1
  2.4 1.0 copy-done.1
  3.5 0.0 copy-start.2
  3.5 0.9 copy-done.2
  4.4 101.0 %shard_map.59 = (f32[128,256]{1,0:T(8,128)S(1)}, f32[16,256]{1,0:T(8,128)S(1)}) custom-call(f32[128,1024]{1,0:T(8,128)S(1)} %bitcast.9, f32[128,1024]{1,0:T(8,128)S(1)} %bitcast.10, f32[128,256]{1,0:T(8,128)S(1)} %bitcast.11, s32[8,128]{1,0:T(8,128)S(1)} %broadcast_in_dim.18.req_ref), custom_call_target="tpu_custom_call" | custom-call | flops 1207959552 | bytes 2097152 | tf_op jit(solution)/shard_map/pallas_call | solution.py:639
  105.4 0.7 copy.9
  106.1 0.6 copy.10
  (2 shorter events, 0.0 us)
Async XLA Ops:
  0.6 0.7 copy-start.3
  1.4 1.0 copy-start
  2.4 1.0 copy-start.1
  3.5 0.9 copy-start.2

commit v4 on v3

--- a/solution.py
+++ b/solution.py
@@ -642,7 +642,7 @@
             jax.ShapeDtypeStruct((rows, total), f32),
             jax.ShapeDtypeStruct((mine, total), f32),
         ),
-        in_specs=[pl.BlockSpec(memory_space=pl.ANY)] * 3 + [pl.BlockSpec(memory_space=vmem)],
+        in_specs=[pl.BlockSpec(memory_space=pltpu.HBM)] * 3 + [pl.BlockSpec(memory_space=vmem)],
         out_specs=(pl.BlockSpec(memory_space=vmem), pl.BlockSpec(memory_space=vmem)),
         scratch_shapes=[
             vmem((count, rows, order), f32),
@@ -693,7 +693,7 @@
             dma((count,)),
         ],
         compiler_params=pltpu.CompilerParams(
-            collective_id=0, has_side_effects=True, vmem_limit_bytes=48 * 2**20
+            collective_id=0, has_side_effects=True, vmem_limit_bytes=62 * 2**20
         ),
         cost_estimate=pl.CostEstimate(
             flops=36 * order * order * cols, bytes_accessed=16 * rows * order, transcendentals=0

time: 107 us -> 106 us (level)
  local copies, waits for them, and re-layouts: 4.98 us -> 3.5 us
    unnamed x10 -> x6, local copies, waits for them, and re-layouts: 4.89 us -> 2.82 us
    pallas_call x1, Pallas kernels: 101 us -> 102 us  [per_device(): pl.pallas_call(sweep_kernel, out_shape=(jax.ShapeDtypeStruct((rows, total...]
where the time goes in v4:
time: 106 us
  Pallas kernels  102 us (96%)
  local copies, waits for them, and re-layouts  3.5 us (3%)
    pallas_call x1, Pallas kernels, per_device(): pl.pallas_call(sweep_kernel, out_shape=(jax.ShapeDtypeStruct((rows, total...  102 us
    unnamed x6, local copies, waits for them, and re-layouts  2.82 us

profile of v4, /device:TPU:0, one launch (start us, length us, event | category | flops | bytes accessed | tf_op | source)
XLA Modules:
  0.0 106.3 jit_solution(1001934169271611281)
XLA Ops:
  0.6 0.0 copy-start.1
  0.7 0.6 copy-done.1
  1.3 0.1 bitcast_dynamic-update-slice_fusion
  1.4 0.6 broadcast_in_dim.18.req_ref
  2.0 102.1 %shard_map.59 = (f32[128,256]{1,0:T(8,128)}, f32[16,256]{1,0:T(8,128)}) custom-call(f32[128,1024]{1,0:T(8,128)} %bitcast.9, f32[128,1024]{1,0:T(8,128)} %bitcast.10, f32[128,256]{1,0:T(8,128)} %bitcast.11, s32[8,128]{1,0:T(8,128)} %broadcast_in_dim.18.req_ref), custom_call_target="tpu_custom_call" | custom-call | flops 1207959552 | bytes 2097152 | tf_op jit(solution)/shard_map/pallas_call | solution.py:639
  104.1 0.0 copy-start
  104.1 1.6 %copy.9 = f32[1,128,256]{2,1,0:T(8,128)} copy(f32[1,128,256]{2,1,0:T(8,128)} %bitcast.7) | data formatting | bytes 262144
  105.7 0.0 copy-done
  105.7 0.6 copy.10
  (1 shorter events, 0.0 us)
Async XLA Ops:
  0.6 0.7 copy-start.1
  104.1 1.6 %copy-start = (f32[16,256]{1,0:T(8,128)S(1)}, f32[16,256]{1,0:T(8,128)}, u32[]{:S(2)}) copy-start(f32[16,256]{1,0:T(8,128)} %get-tuple-element.5) | copy-start | bytes 49156
